TPU v7x, 32 devices: a whole 2x2x4 slice. The times are simulated.
32 devices in a mesh: dp: 4 (over z), expert: 4 (over y, x), tensor: 2 (over core).
Axes of the slice: x: 2, y: 2, z: 4, core: 2. Of those that a mesh axis runs over, the one named last changes fastest.
Arguments:
- hidden_in: bfloat16 [4096, 2048], P(('dp', 'expert')), may hold values from -6 to 6
- query: bfloat16 [4096, 2048], P(('dp', 'expert'), 'tensor'), may hold values from -26 to 26
- keys: bfloat16 [4096, 2048], P(('dp', 'expert'), 'tensor'), may hold values from -26 to 26
- values: bfloat16 [4096, 2048], P(('dp', 'expert'), 'tensor'), may hold values from -6 to 6
- out_proj: bfloat16 [2048, 2048], P('tensor'), may hold values from -0.125 to 0.125
- norm_gain: bfloat16 [2048], replicated, may hold values from 0.25 to 1.75
- routes: int32 [4096, 2], P(('dp', 'expert')), may hold values from 0 to 3, all different within a row; in each aligned block of 256 rows (0 to 255, 256 to 511, ...) at most 144 rows name the same one
- gates: float32 [4096, 2], P(('dp', 'expert')), may hold values from 0.2 to 1
- w_gate: bfloat16 [4, 2048, 5504], P('expert', 'dp', 'tensor'), may hold values from -0.125 to 0.125
- w_up: bfloat16 [4, 2048, 5504], P('expert', 'dp', 'tensor'), may hold values from -0.125 to 0.125
- w_down_t: bfloat16 [4, 2048, 5504], P('expert', 'dp', 'tensor'), may hold values from -0.078125 to 0.078125
Outputs:
- layer_out: bfloat16 [4096, 2048], P(('dp', 'expert'), 'tensor')
Inputs may be any that keep to these rules, and one draw needn't show every extreme that they name: `routes`: each row names 2 different experts; in the 256 rows of one block of consecutive tokens no expert is named more than 144 times, a bound that some block reaches.
All inputs are finite; a program needn't handle non-finite values.
Results may differ from a plain program's by a relative error of at most 0.0095.
Values may be sent and summed in bfloat16 or wider, within the bound.
A program may use at most 128 MiB of HBM per device.

v0:
```python
import jax
import jax.numpy as jnp
from jax import lax
from jax.sharding import PartitionSpec as P

HDIM = 128


EPSILON = 1e-05
NEGATIVE = -1e30


def slot_table(block_routes, experts, capacity):
    flat_routes = block_routes.reshape(-1)
    pairs = flat_routes.shape[0]
    onehot = flat_routes[:, None] == jnp.arange(experts, dtype=jnp.int32)[None, :]
    order = jnp.arange(pairs, dtype=jnp.int32)
    earlier = (order[:, None] > order[None, :]).astype(jnp.bfloat16)
    rank_table = jnp.dot(
        earlier, onehot.astype(jnp.bfloat16), preferred_element_type=jnp.float32
    )
    slot_index = jnp.sum(jnp.where(onehot, rank_table, 0.0), axis=1).astype(jnp.int32)
    return flat_routes * capacity + slot_index


def attention(query, both, score_scale):
    tok_rows, head_cols = query.shape
    head_count = head_cols // HDIM
    query_pos = lax.axis_index("expert") * tok_rows + jnp.arange(tok_rows, dtype=jnp.int32)
    key_rows, value_rows = both[:, :head_cols], both[:, head_cols:]
    count_rows = key_rows.shape[0]
    key_pos = jnp.arange(count_rows, dtype=jnp.int32)
    queries = query.reshape(tok_rows, head_count, HDIM)
    key_part = key_rows.reshape(count_rows, head_count, HDIM)
    value_part = value_rows.reshape(count_rows, head_count, HDIM)
    scores = (
        jnp.einsum("qhd,khd->hqk", queries, key_part, preferred_element_type=jnp.float32)
        * score_scale
    )
    causal = (query_pos[:, None] >= key_pos[None, :])[None]
    scores = jnp.where(causal, scores, NEGATIVE)
    new_max = jnp.max(scores, axis=-1)
    weights_now = jnp.where(causal, jnp.exp(scores - new_max[..., None]), 0.0)
    totals = jnp.sum(weights_now, axis=-1)
    weighted = jnp.einsum("hqk,khd->hqd", weights_now, value_part.astype(jnp.float32))
    context = weighted / totals[..., None]
    return jnp.transpose(context, (1, 0, 2)).reshape(tok_rows, head_cols).astype(jnp.bfloat16)


def local(
    hidden_in, query, keys, values, out_proj, norm_gain, routes, gates, w_gate, w_up, w_down_t
):
    tok_rows, feature_width = hidden_in.shape
    top = routes.shape[1]
    experts = lax.axis_size("expert")
    copies = lax.axis_size("dp")
    capacity = 9 * tok_rows // (4 * experts)
    slots = experts * capacity
    tensor_count = lax.axis_size("tensor")
    slice_width = feature_width // tensor_count
    tensor_index = lax.axis_index("tensor")
    shard_rows, hidden_width = w_gate.shape[1:]
    exchange = 2 * tok_rows * feature_width < 3 * shard_rows * hidden_width and copies <= 4
    if hidden_width % copies:
        exchange = False

    def spread(w):
        if not exchange:
            return lax.all_gather(w[0], "dp", axis=0, tiled=True)
        share = hidden_width // copies
        me = lax.axis_index("dp")
        turned = jnp.transpose(w[0]).reshape(copies, share, shard_rows)
        blocks = []
        for step in range(copies):
            block = lax.dynamic_index_in_dim(turned, (me + step) % copies, 0, keepdims=False)
            if step:
                block = lax.ppermute(
                    block, "dp", [(i, (i + step) % copies) for i in range(copies)]
                )
            blocks.append(block)
        stacked = jnp.stack(blocks)
        ordered = [
            lax.dynamic_index_in_dim(stacked, (me - i + copies) % copies, 0, keepdims=False)
            for i in range(copies)
        ]
        return jnp.transpose(jnp.concatenate(ordered, axis=1))

    gate_full, up_full, down_full = spread(w_gate), spread(w_up), spread(w_down_t)

    choice = jnp.concatenate([routes.astype(jnp.float32), gates], axis=1)
    both = lax.all_gather(jnp.concatenate([keys, values], axis=1), "expert", axis=0, tiled=True)
    if exchange:
        choice = lax.all_gather(choice, "dp", axis=0)
        both, choice, gate_full = lax.optimization_barrier((both, choice, gate_full))
    else:
        choice = choice[None]
    context = attention(query, both, 1.0 / HDIM**0.5)
    attended = lax.psum(
        jnp.dot(context, out_proj, preferred_element_type=jnp.float32).astype(jnp.bfloat16),
        "tensor",
    )
    if exchange:
        attended, up_full = lax.optimization_barrier((attended, up_full))
    attended = attended.astype(jnp.float32)
    residual = hidden_in.astype(jnp.float32) + attended
    mean_square = jnp.mean(residual * residual, axis=-1, keepdims=True)
    normed = (residual * lax.rsqrt(mean_square + EPSILON) * norm_gain.astype(jnp.float32)).astype(
        jnp.bfloat16
    )
    own_cols = lax.dynamic_slice_in_dim(normed, tensor_index * slice_width, slice_width, 1)
    own_slice = lax.dynamic_slice_in_dim(residual, tensor_index * slice_width, slice_width, 1)
    blocks = lax.all_gather(own_cols, "dp", axis=0) if exchange else own_cols[None]
    count = blocks.shape[0]
    sends, mixers = [], []
    slot_numbers = jnp.arange(slots, dtype=jnp.int32)[:, None]
    for i in range(count):
        picked = choice[i, :, :top].astype(jnp.int32)
        targets = slot_table(picked, experts, capacity).reshape(tok_rows, top)
        place = jnp.zeros((slots, tok_rows), jnp.float32)
        mixing = jnp.zeros((slots, tok_rows), jnp.float32)
        for k in range(top):
            chosen = slot_numbers == targets[:, k][None, :]
            place = jnp.where(chosen, 1.0, place)
            mixing = jnp.where(chosen, choice[i, :, top + k][None, :], mixing)
        sent = jnp.dot(
            place.astype(jnp.bfloat16), blocks[i], preferred_element_type=jnp.float32
        ).astype(jnp.bfloat16)
        sends.append(sent.reshape(experts, capacity, slice_width))
        mixers.append(mixing)
    arrived = lax.all_to_all(
        jnp.concatenate(sends, axis=1), "expert", split_axis=0, concat_axis=0, tiled=True
    ).reshape(count * slots, slice_width)
    if exchange:
        arrived, down_full = lax.optimization_barrier((arrived, down_full))
    halves = lax.all_gather(arrived, "tensor", axis=0)
    slot_rows = jnp.concatenate([halves[i] for i in range(tensor_count)], axis=1)
    gate_out = jnp.dot(slot_rows, gate_full, preferred_element_type=jnp.float32)
    up_out = jnp.dot(slot_rows, up_full, preferred_element_type=jnp.float32)
    hidden = (jax.nn.silu(gate_out) * up_out).astype(jnp.bfloat16)
    rounded = lax.dot_general(
        hidden, down_full, (((1,), (1,)), ((), ())), preferred_element_type=jnp.float32
    ).astype(jnp.bfloat16)
    summed = lax.psum_scatter(rounded, "tensor", scatter_dimension=1, tiled=True)
    returned = lax.all_to_all(
        summed.reshape(experts, count * capacity, slice_width),
        "expert",
        split_axis=0,
        concat_axis=0,
        tiled=True,
    )
    mixtures = []
    for i in range(count):
        rows = returned[:, i * capacity : (i + 1) * capacity].reshape(slots, slice_width)
        high = lax.reduce_precision(mixers[i], 8, 7)
        mixtures.append(
            sum(
                lax.dot_general(
                    term.astype(jnp.bfloat16),
                    rows,
                    (((0,), (0,)), ((), ())),
                    preferred_element_type=jnp.float32,
                )
                for term in (high, mixers[i] - high)
            )
        )
    if exchange:
        mixture = lax.psum_scatter(
            jnp.concatenate(mixtures, axis=0).astype(jnp.bfloat16),
            "dp",
            scatter_dimension=0,
            tiled=True,
        ).astype(jnp.float32)
    else:
        mixture = mixtures[0]
    return (own_slice + mixture).astype(jnp.bfloat16)


def solution(mesh):
    in_specs = (
        P(("dp", "expert"), None),
        P(("dp", "expert"), "tensor"),
        P(("dp", "expert"), "tensor"),
        P(("dp", "expert"), "tensor"),
        P("tensor", None),
        P(),
        P(("dp", "expert"), None),
        P(("dp", "expert"), None),
        P("expert", "dp", "tensor"),
        P("expert", "dp", "tensor"),
        P("expert", "dp", "tensor"),
    )
    out_specs = P(("dp", "expert"), "tensor")
    return jax.shard_map(local, mesh=mesh, in_specs=in_specs, out_specs=out_specs, check_vma=False)
```

profile of v0, /device:TPU:0, one launch (start us, length us, event | category | flops | bytes accessed | tf_op | source)
XLA Modules:
  0.0 506.4 jit_solution(8007738320580794210)
XLA Ops:
  10.3 3.3 constant_dynamic-slice_fusion.2
  13.6 5.0 collective-permute-start.2
  21.1 2.8 collective-permute-start.5
  25.0 107.1 %all-gather = f32[1024,4]{0,1:T(4,128)S(1)} all-gather(f32[256,4]{0,1:T(4,128)S(1)} %pad_maximum_fusion.13), channel_id=2, replica_groups=mesh['dp'=4,'expert'=4,'tensor'=2] {'dp'}, dimensions={0}, use_global_device_ids=true | all-gather | bytes 20480 | tf_op jit(solution)/shard_map/all_gather | solution.py:93
  136.4 2.7 fusion.124
  140.8 2.0 fusion.3
  142.8 2.3 divide_convert_fusion
  145.1 2.3 convolution_convert_fusion.1
  153.2 15.5 %all-reduce.2.cloned.1.call-done = bf16[256,2048]{1,0:T(8,128)(2,1)} async-done(((bf16[256,2048]{1,0:T(8,128)(2,1)}), bf16[256,2048]{1,0:T(8,128)(2,1)}) %all-reduce.2.cloned.1.call-update) | async-done | bytes 1048592 | tf_op jit(solution)/shard_map/psum | solution.py:98
  176.2 42.7 %all-gather.9.cloned.1.call-done = bf16[1024,1024]{1,0:T(8,128)(2,1)} async-done(((bf16[256,1024]{1,0:T(8,128)(2,1)}), bf16[1024,1024]{1,0:T(8,128)(2,1)}) %all-gather.9.cloned.1.call-update) | async-done | bytes 2097168 | tf_op jit(solution)/shard_map/all_gather | solution.py:112
  223.1 2.4 pad_maximum_fusion.3
  225.5 4.9 all-to-all-start
  235.5 15.5 %collective-permute-done.8 = bf16[688,512]{1,0:T(8,128)(2,1)S(1)} collective-permute-done((bf16[688,512]{1,0:T(8,128)(2,1)S(1)}, bf16[688,512]{1,0:T(8,128)(2,1)S(1)}, u32[]{:S(2)}, u32[]{:S(2)}) %collective-permute-start.8) | collective-permute-done | bytes 704544 | tf_op jit(solution)/shard_map/ppermute | solution.py:77
  251.0 43.6 %collective-permute-done.7 = bf16[688,512]{1,0:T(8,128)(2,1)S(1)} collective-permute-done((bf16[688,512]{1,0:T(8,128)(2,1)S(1)}, bf16[688,512]{1,0:T(8,128)(2,1)S(1)}, u32[]{:S(2)}, u32[]{:S(2)}) %collective-permute-start.7) | collective-permute-done | bytes 704544 | tf_op jit(solution)/shard_map/ppermute | solution.py:77
  297.0 22.7 %all-gather.11.cloned.1.call-done = bf16[4608,1024]{1,0:T(8,128)(2,1)} async-done(((bf16[2304,1024]{1,0:T(8,128)(2,1)}), bf16[4608,1024]{1,0:T(8,128)(2,1)}) %all-gather.11.cloned.1.call-update) | async-done | bytes 9437200 | tf_op jit(solution)/shard_map/all_gather | solution.py:135
  319.7 7.0 %fusion.122 = (bf16[2304,1024]{1,0:T(8,128)(2,1)S(1)}, bf16[2304,1024]{1,0:T(8,128)(2,1)}) fusion(bf16[4608,1024]{1,0:T(8,128)(2,1)} %all-gather.11.cloned.1.call-done), kind=kLoop, calls=%fused_computation.230 | loop fusion | bytes 18874368 | tf_op jit(solution)/shard_map/slice | solution.py:136
  326.7 2.1 copy-done.2
  328.8 12.0 %fusion.2 = f32[2304,688]{0,1:T(8,128)} fusion(bf16[2048,688]{0,1:T(8,128)(2,1)} %maximum_bitcast_fusion, bf16[2304,1024]{1,0:T(8,128)(2,1)} %get-tuple-element.36, bf16[2304,1024]{1,0:T(8,128)(2,1)S(1)} %get-tuple-element.35), kind=kOutput, calls=%fused_computation.7 | convolution fusion | flops 6511656960 | bytes 18595840 | tf_op jit(solution)/shard_map/dot_general | solution.py:137
  340.8 25.1 %convolution_convert_fusion = bf16[2304,2048]{1,0:T(8,128)(2,1)} fusion(bf16[2048,688]{0,1:T(8,128)(2,1)} %maximum_bitcast_fusion.2, f32[2304,688]{0,1:T(8,128)} %fusion.2, bf16[2048,688]{0,1:T(8,128)(2,1)} %maximum_bitcast_fusion.1, bf16[2304,1024]{1,0:T(8,128)(2,1)} %get-tuple-element.36, bf16[2304,1024]{1,0:T(8,128)(2,1)} %copy-done.2), kind=kOutput, calls=%fused_computation | convolution fusion | flops 13018669056 | bytes 30851072 | tf_op jit(solution)/shard_map/dot_general | solution.py:140
  365.9 19.1 %reduce-scatter.3.cloned.1.call-done = bf16[2304,1024]{1,0:T(8,128)(2,1)} async-done(((bf16[2304,2048]{1,0:T(8,128)(2,1)}), bf16[2304,1024]{1,0:T(8,128)(2,1)}) %reduce-scatter.3.cloned.1.call-update) | async-done | bytes 4718608 | tf_op jit(solution)/shard_map/reduce_scatter | solution.py:143
  385.1 4.9 all-to-all-start.1
  391.0 52.8 %all-to-all-done.1 = bf16[4,576,1024]{2,1,0:T(8,128)(2,1)} async-done(((bf16[4,576,1024]{2,1,0:T(8,128)(2,1)}), bf16[4,576,1024]{2,1,0:T(8,128)(2,1)}, u32[]{:S(2)}, u32[]{:S(2)}) %all-to-all-start.1) | async-done | bytes 4718624 | tf_op jit(solution)/shard_map/all_to_all | solution.py:144
  443.8 2.9 fusion.123
  453.3 44.2 %reduce-scatter.5.cloned.1.call-done = bf16[256,1024]{1,0:T(8,128)(2,1)} async-done(((bf16[1024,1024]{1,0:T(8,128)(2,1)}), bf16[256,1024]{1,0:T(8,128)(2,1)}) %reduce-scatter.5.cloned.1.call-update) | async-done | bytes 524304 | tf_op jit(solution)/shard_map/reduce_scatter | solution.py:167
  (104 shorter events, 47.5 us)
Async XLA Ops:
  6.5 132.5 %copy-start = (bf16[256,1024]{1,0:T(8,128)(2,1)S(1)}, bf16[256,1024]{1,0:T(8,128)(2,1)}, u32[]{:S(2)}) copy-start(bf16[256,1024]{1,0:T(8,128)(2,1)} %param.12) | copy-start | bytes 1572868
  6.5 129.8 %all-gather.7.cloned.1.call-start = ((), (), s32[]{:S(2)}) async-start(), calls=%async_computation.4 | async-start | bytes 5242880 | tf_op jit(solution)/shard_map/all_gather | solution.py:91
  10.2 158.5 %all-reduce.2.cloned.1.call-start = ((), (), s32[]{:S(2)}) async-start(), calls=%async_computation.5 | async-start | bytes 2097152 | tf_op jit(solution)/shard_map/psum | solution.py:98
  10.3 9.4 %copy-start.3 = (bf16[1,512,2752]{1,2,0:T(8,128)(2,1)S(1)}, bf16[1,512,2752]{1,2,0:T(8,128)(2,1)}, u32[]{:S(2)}) copy-start(bf16[1,512,2752]{1,2,0:T(8,128)(2,1)} %param.20) | copy-start | bytes 8454148
  13.6 118.9 %collective-permute-start.2 = (bf16[688,512]{1,0:T(8,128)(2,1)}, bf16[688,512]{1,0:T(8,128)(2,1)}, u32[]{:S(2)}, u32[]{:S(2)}) collective-permute-start(bf16[688,512]{1,0:T(8,128)(2,1)} %get-tuple-element.64), channel_id=1, source_target_pairs={{0,24},{8,0},{16,8},{24,16},{1,25},{9,1},{17,9},{25,17},{2,26},{10... | collective-permute-start | bytes 2113544 | tf_op jit(solution)/shard_map/ppermute | solution.py:77
  18.7 113.9 %collective-permute-start.1 = (bf16[688,512]{1,0:T(8,128)(2,1)}, bf16[688,512]{1,0:T(8,128)(2,1)}, u32[]{:S(2)}, u32[]{:S(2)}) collective-permute-start(bf16[688,512]{1,0:T(8,128)(2,1)} %get-tuple-element.65), channel_id=1, source_target_pairs={{0,16},{8,24},{16,0},{24,8},{1,17},{9,25},{17,1},{25,9},{2,18},{10... | collective-permute-start | bytes 2113544 | tf_op jit(solution)/shard_map/ppermute | solution.py:77
  18.7 113.9 %collective-permute-start = (bf16[688,512]{1,0:T(8,128)(2,1)}, bf16[688,512]{1,0:T(8,128)(2,1)}, u32[]{:S(2)}, u32[]{:S(2)}) collective-permute-start(bf16[688,512]{1,0:T(8,128)(2,1)} %get-tuple-element.66), channel_id=1, source_target_pairs={{0,8},{8,16},{16,24},{24,0},{1,9},{9,17},{17,25},{25,1},{2,10},{10... | collective-permute-start | bytes 2113544 | tf_op jit(solution)/shard_map/ppermute | solution.py:77
  19.7 5.3 %copy-start.5 = (s32[256,2]{0,1:T(2,128)S(1)}, s32[256,2]{0,1:T(2,128)}, u32[]{:S(2)}) copy-start(s32[256,2]{0,1:T(2,128)} %param.17) | copy-start | bytes 6148
  19.7 5.3 %copy-start.6 = (f32[256,2]{0,1:T(2,128)S(1)}, f32[256,2]{0,1:T(2,128)}, u32[]{:S(2)}) copy-start(f32[256,2]{0,1:T(2,128)} %param.18) | copy-start | bytes 6148
  21.1 126.7 %collective-permute-start.5 = (bf16[688,512]{1,0:T(8,128)(2,1)}, bf16[688,512]{1,0:T(8,128)(2,1)}, u32[]{:S(2)}, u32[]{:S(2)}) collective-permute-start(bf16[688,512]{1,0:T(8,128)(2,1)} %get-tuple-element.56), channel_id=1, source_target_pairs={{0,24},{8,0},{16,8},{24,16},{1,25},{9,1},{17,9},{25,17},{2,26},{10... | collective-permute-start | bytes 2113544 | tf_op jit(solution)/shard_map/ppermute | solution.py:77
  23.9 123.9 %collective-permute-start.4 = (bf16[688,512]{1,0:T(8,128)(2,1)}, bf16[688,512]{1,0:T(8,128)(2,1)}, u32[]{:S(2)}, u32[]{:S(2)}) collective-permute-start(bf16[688,512]{1,0:T(8,128)(2,1)} %get-tuple-element.57), channel_id=1, source_target_pairs={{0,16},{8,24},{16,0},{24,8},{1,17},{9,25},{17,1},{25,9},{2,18},{10... | collective-permute-start | bytes 2113544 | tf_op jit(solution)/shard_map/ppermute | solution.py:77
  132.5 16.8 %collective-permute-start.3 = (bf16[688,512]{1,0:T(8,128)(2,1)S(1)}, bf16[688,512]{1,0:T(8,128)(2,1)}, u32[]{:S(2)}, u32[]{:S(2)}) collective-permute-start(bf16[688,512]{1,0:T(8,128)(2,1)S(1)} %get-tuple-element.58), channel_id=1, source_target_pairs={{0,8},{8,16},{16,24},{24,0},{1,9},{9,17},{17,25},{25,1},{2,10},{10... | collective-permute-start | bytes 2113544 | tf_op jit(solution)/shard_map/ppermute | solution.py:77
  145.1 2.6 copy-start.4
  147.5 71.4 %all-gather.9.cloned.1.call-start = ((), (), s32[]{:S(2)}) async-start(), calls=%async_computation.8 | async-start | bytes 2621440 | tf_op jit(solution)/shard_map/all_gather | solution.py:112
  218.9 3.2 copy-start.8
  225.5 71.5 %all-to-all-start = ((bf16[4,576,1024]{2,1,0:T(8,128)(2,1)}), bf16[4,576,1024]{2,1,0:T(8,128)(2,1)}, u32[]{:S(2)}, u32[]{:S(2)}) async-start(bf16[4,576,1024]{2,1,0:T(8,128)(2,1)} %pad_maximum_fusion.3), calls=%async_computation | async-start | bytes 9437184 | tf_op jit(solution)/shard_map/all_to_all | solution.py:130
  230.4 89.3 %all-gather.11.cloned.1.call-start = ((), (), s32[]{:S(2)}) async-start(), calls=%async_computation.9 | async-start | bytes 14155776 | tf_op jit(solution)/shard_map/all_gather | solution.py:135
  232.4 18.6 %collective-permute-start.8 = (bf16[688,512]{1,0:T(8,128)(2,1)S(1)}, bf16[688,512]{1,0:T(8,128)(2,1)S(1)}, u32[]{:S(2)}, u32[]{:S(2)}) collective-permute-start(bf16[688,512]{1,0:T(8,128)(2,1)S(1)} %get-tuple-element.48), channel_id=1, source_target_pairs={{0,24},{8,0},{16,8},{24,16},{1,25},{9,1},{17,9},{25,17},{2,26},{10... | collective-permute-start | bytes 2113544 | tf_op jit(solution)/shard_map/ppermute | solution.py:77
  233.6 61.0 %collective-permute-start.7 = (bf16[688,512]{1,0:T(8,128)(2,1)S(1)}, bf16[688,512]{1,0:T(8,128)(2,1)S(1)}, u32[]{:S(2)}, u32[]{:S(2)}) collective-permute-start(bf16[688,512]{1,0:T(8,128)(2,1)S(1)} %get-tuple-element.49), channel_id=1, source_target_pairs={{0,16},{8,24},{16,0},{24,8},{1,17},{9,25},{17,1},{25,9},{2,18},{10... | collective-permute-start | bytes 2113544 | tf_op jit(solution)/shard_map/ppermute | solution.py:77
  233.8 60.8 %collective-permute-start.6 = (bf16[688,512]{1,0:T(8,128)(2,1)S(1)}, bf16[688,512]{1,0:T(8,128)(2,1)S(1)}, u32[]{:S(2)}, u32[]{:S(2)}) collective-permute-start(bf16[688,512]{1,0:T(8,128)(2,1)S(1)} %get-tuple-element.50), channel_id=1, source_target_pairs={{0,8},{8,16},{16,24},{24,0},{1,9},{9,17},{17,25},{25,1},{2,10},{10... | collective-permute-start | bytes 2113544 | tf_op jit(solution)/shard_map/ppermute | solution.py:77
  297.0 88.1 %reduce-scatter.3.cloned.1.call-start = ((), (), s32[]{:S(2)}) async-start(), calls=%async_computation.6 | async-start | bytes 14155776 | tf_op jit(solution)/shard_map/reduce_scatter | solution.py:143
  385.1 58.7 %all-to-all-start.1 = ((bf16[4,576,1024]{2,1,0:T(8,128)(2,1)}), bf16[4,576,1024]{2,1,0:T(8,128)(2,1)}, u32[]{:S(2)}, u32[]{:S(2)}) async-start(bf16[4,576,1024]{2,1,0:T(8,128)(2,1)} %bitcast.140), calls=%async_computation.2 | async-start | bytes 9437184 | tf_op jit(solution)/shard_map/all_to_all | solution.py:144
  390.0 107.6 %reduce-scatter.5.cloned.1.call-start = ((), (), s32[]{:S(2)}) async-start(), calls=%async_computation.7 | async-start | bytes 2621440 | tf_op jit(solution)/shard_map/reduce_scatter | solution.py:167
  451.8 47.8 %copy-start.1 = (bf16[256,1024]{1,0:T(8,128)(2,1)S(1)}, bf16[256,1024]{1,0:T(8,128)(2,1)}, u32[]{:S(2)}) copy-start(bf16[256,1024]{1,0:T(8,128)(2,1)} %param.12) | copy-start | bytes 1572868
  (2 other events, 4.4 us)
Sparse Core Ops, SparseCore 0:
  10.3 55.2 all-gather.6
  147.6 21.0 all-reduce.1
  171.8 47.1 all-gather.8
  297.1 22.5 all-gather.10
  366.1 18.9 reduce-scatter.2
  453.5 44.0 reduce-scatter.4
where the time goes:
time: 507 us; the launch traced here: 506 us
  waiting for transfers between devices  258 us (51%)
  blocking collectives  107 us (21%)
  matrix products  53.7 us (11%)
  local copies, waits for them, and re-layouts  27.8 us (5%)
  starting transfers between devices  23.7 us (5%)
  other arithmetic  22.4 us (4%)
  between operations  14 us (3%)
    all_gather x1, blocking collectives, local(): choice = lax.all_gather(choice, 'dp', axis=0)  107 us
    ppermute x9, waiting for transfers between devices, spread(): lax.ppermute(block, 'dp', [(i, (i + step) % copies) for i in range(copies)])  60.6 us
    all_to_all x1, waiting for transfers between devices, local(): lax.all_to_all(summed.reshape(experts, count * capacity, slice_width), 'e...  52.8 us
    reduce_scatter x1, waiting for transfers between devices, local(): lax.psum_scatter(jnp.concatenate(mixtures, axis=0).astype(jnp.bfloat16),...  44.2 us
    all_gather x1, waiting for transfers between devices, local(): lax.all_gather(own_cols, 'dp', axis=0)  42.7 us
    dot_general x1, matrix products, local(): lax.dot_general(hidden, down_full, (((1,), (1,)), ((), ())), preferred_el...  25.1 us
    all_gather x1, waiting for transfers between devices, local(): halves = lax.all_gather(arrived, 'tensor', axis=0)  22.7 us
    reduce_scatter x1, waiting for transfers between devices, local(): lax.psum_scatter(rounded, 'tensor', scatter_dimension=1, tiled=True)  19.1 us
  transfers between devices with their start and end apart: 17, of which 9 were waited for; matrix products, arithmetic and copies ran while one was open for 7% of the time, Pallas kernels for 0%

commit v1 on v0

--- a/solution.py
+++ b/solution.py
@@ -85,15 +85,18 @@
         ]
         return jnp.transpose(jnp.concatenate(ordered, axis=1))
 
-    gate_full, up_full, down_full = spread(w_gate), spread(w_up), spread(w_down_t)
-
     choice = jnp.concatenate([routes.astype(jnp.float32), gates], axis=1)
     both = lax.all_gather(jnp.concatenate([keys, values], axis=1), "expert", axis=0, tiled=True)
     if exchange:
         choice = lax.all_gather(choice, "dp", axis=0)
-        both, choice, gate_full = lax.optimization_barrier((both, choice, gate_full))
+        choice, w_gate, w_up, w_down_t = lax.optimization_barrier(
+            (choice, w_gate, w_up, w_down_t)
+        )
     else:
         choice = choice[None]
+    gate_full, up_full, down_full = spread(w_gate), spread(w_up), spread(w_down_t)
+    if exchange:
+        both, gate_full = lax.optimization_barrier((both, gate_full))
     context = attention(query, both, 1.0 / HDIM**0.5)
     attended = lax.psum(
         jnp.dot(context, out_proj, preferred_element_type=jnp.float32).astype(jnp.bfloat16),
@@ -137,41 +140,52 @@
     gate_out = jnp.dot(slot_rows, gate_full, preferred_element_type=jnp.float32)
     up_out = jnp.dot(slot_rows, up_full, preferred_element_type=jnp.float32)
     hidden = (jax.nn.silu(gate_out) * up_out).astype(jnp.bfloat16)
-    rounded = lax.dot_general(
-        hidden, down_full, (((1,), (1,)), ((), ())), preferred_element_type=jnp.float32
-    ).astype(jnp.bfloat16)
-    summed = lax.psum_scatter(rounded, "tensor", scatter_dimension=1, tiled=True)
-    returned = lax.all_to_all(
-        summed.reshape(experts, count * capacity, slice_width),
-        "expert",
-        split_axis=0,
-        concat_axis=0,
-        tiled=True,
-    )
-    mixtures = []
-    for i in range(count):
-        rows = returned[:, i * capacity : (i + 1) * capacity].reshape(slots, slice_width)
-        high = lax.reduce_precision(mixers[i], 8, 7)
-        mixtures.append(
-            sum(
-                lax.dot_general(
-                    term.astype(jnp.bfloat16),
-                    rows,
-                    (((0,), (0,)), ((), ())),
-                    preferred_element_type=jnp.float32,
+    hidden = lax.optimization_barrier(hidden)
+    parts = 2 if slice_width % 256 == 0 else 1
+    width = slice_width // parts
+    down_parts = down_full.reshape(tensor_count, parts, width, down_full.shape[1])
+    splits = [(mixing, lax.reduce_precision(mixing, 8, 7)) for mixing in mixers]
+    pieces = []
+    for part in range(parts):
+        rounded = lax.dot_general(
+            hidden,
+            down_parts[:, part].reshape(tensor_count * width, down_full.shape[1]),
+            (((1,), (1,)), ((), ())),
+            preferred_element_type=jnp.float32,
+        ).astype(jnp.bfloat16)
+        summed = lax.psum_scatter(rounded, "tensor", scatter_dimension=1, tiled=True)
+        returned = lax.all_to_all(
+            summed.reshape(experts, count * capacity, width),
+            "expert",
+            split_axis=0,
+            concat_axis=0,
+            tiled=True,
+        )
+        mixtures = []
+        for i, (mixing, high) in enumerate(splits):
+            rows = returned[:, i * capacity : (i + 1) * capacity].reshape(slots, width)
+            mixtures.append(
+                sum(
+                    lax.dot_general(
+                        term.astype(jnp.bfloat16),
+                        rows,
+                        (((0,), (0,)), ((), ())),
+                        preferred_element_type=jnp.float32,
+                    )
+                    for term in (high, mixing - high)
                 )
-                for term in (high, mixers[i] - high)
             )
-        )
-    if exchange:
-        mixture = lax.psum_scatter(
-            jnp.concatenate(mixtures, axis=0).astype(jnp.bfloat16),
-            "dp",
-            scatter_dimension=0,
-            tiled=True,
-        ).astype(jnp.float32)
-    else:
-        mixture = mixtures[0]
+        if exchange:
+            piece = lax.psum_scatter(
+                jnp.concatenate(mixtures, axis=0).astype(jnp.bfloat16),
+                "dp",
+                scatter_dimension=0,
+                tiled=True,
+            ).astype(jnp.float32)
+        else:
+            piece = mixtures[0]
+        pieces.append(piece)
+    mixture = jnp.concatenate(pieces, axis=1)
     return (own_slice + mixture).astype(jnp.bfloat16)
 
 

time: 507 us -> 479 us (0.945); the launches traced: 506 us -> 471 us
  blocking collectives: 107 us -> 14.8 us
  starting transfers between devices: 23.7 us -> 54.5 us
  local copies, waits for them, and re-layouts: 27.8 us -> 56.1 us
    all_gather x1, blocking collectives: 107 us -> 14.8 us  [local(): choice = lax.all_gather(choice, 'dp', axis=0)]
    ppermute x9, waiting for transfers between devices: 60.6 us -> 127 us  [spread(): lax.ppermute(block, 'dp', [(i, (i + step) % copies) for i in range(copies)])]
    ppermute x9, starting transfers between devices: 13.2 us -> 40.5 us  [spread(): lax.ppermute(block, 'dp', [(i, (i + step) % copies) for i in range(copies)])]
    all_gather x1, waiting for transfers between devices: 22.7 us -> 0.01 us  [local(): halves = lax.all_gather(arrived, 'tensor', axis=0)]
    slice x1 -> x3, local copies, waits for them, and re-layouts: 2.88 us -> 21.4 us  [the longest x1 19.3 us: local(): down_parts[:, part].reshape(tensor_count * width, down_full.shape[1])]
    all_to_all x1 -> x2, waiting for transfers between devices: 52.8 us -> 36.8 us  [local(): lax.all_to_all(summed.reshape(experts, count * capacity, width), 'expert'...]
    psum x1, waiting for transfers between devices: 15.5 us -> 2.8 us  [local(): lax.psum(jnp.dot(context, out_proj, preferred_element_type=jnp.float32).a...]
    reduce_scatter x1 -> x2, waiting for transfers between devices: 44.2 us -> 31.6 us  [local(): lax.psum_scatter(jnp.concatenate(mixtures, axis=0).astype(jnp.bfloat16),...]
  transfers between devices with their start and end apart: 17 -> 20, of which waited for: 9 -> 13; matrix products, arithmetic and copies ran while one was open for 7% -> 16% of each run, Pallas kernels for 0% -> 0%
where the time goes in v1:
time: 479 us; the launch traced here: 471 us
  waiting for transfers between devices  258 us (54%)
  local copies, waits for them, and re-layouts  56.1 us (12%)
  starting transfers between devices  54.5 us (11%)
  matrix products  52.3 us (11%)
  other arithmetic  21.6 us (5%)
  blocking collectives  14.8 us (3%)
  between operations  14.5 us (3%)
    ppermute x9, waiting for transfers between devices, spread(): lax.ppermute(block, 'dp', [(i, (i + step) % copies) for i in range(copies)])  127 us
    all_gather x1, waiting for transfers between devices, local(): lax.all_gather(own_cols, 'dp', axis=0)  44.2 us
    ppermute x9, starting transfers between devices, spread(): lax.ppermute(block, 'dp', [(i, (i + step) % copies) for i in range(copies)])  40.5 us
    all_to_all x2, waiting for transfers between devices, local(): lax.all_to_all(summed.reshape(experts, count * capacity, width), 'expert'...  36.8 us
    reduce_scatter x2, waiting for transfers between devices, local(): lax.psum_scatter(jnp.concatenate(mixtures, axis=0).astype(jnp.bfloat16),...  31.6 us
    slice x1, local copies, waits for them, and re-layouts, local(): down_parts[:, part].reshape(tensor_count * width, down_full.shape[1])  19.3 us
    reduce_scatter x2, waiting for transfers between devices, local(): lax.psum_scatter(rounded, 'tensor', scatter_dimension=1, tiled=True)  15.6 us
    all_gather x1, blocking collectives, local(): choice = lax.all_gather(choice, 'dp', axis=0)  14.8 us
  transfers between devices with their start and end apart: 20, of which 13 were waited for; matrix products, arithmetic and copies ran while one was open for 16% of the time, Pallas kernels for 0%

profile of v1, /device:TPU:0, one launch (start us, length us, event | category | flops | bytes accessed | tf_op | source)
XLA Modules:
  0.0 471.5 jit_solution(1408861958945248297)
XLA Ops:
  10.3 14.8 %all-gather = f32[1024,4]{0,1:T(4,128)S(1)} all-gather(f32[256,4]{0,1:T(4,128)S(1)} %pad_maximum_fusion.12), channel_id=2, replica_groups=mesh['dp'=4,'expert'=4,'tensor'=2] {'dp'}, dimensions={0}, use_global_device_ids=true | all-gather | bytes 20480 | tf_op jit(solution)/shard_map/all_gather | solution.py:91
  38.7 11.5 %collective-permute-done.2 = bf16[688,512]{1,0:T(8,128)(2,1)} collective-permute-done((bf16[688,512]{1,0:T(8,128)(2,1)}, bf16[688,512]{1,0:T(8,128)(2,1)}, u32[]{:S(2)}, u32[]{:S(2)}) %collective-permute-start.2) | collective-permute-done | bytes 704544 | tf_op jit(solution)/shard_map/ppermute | solution.py:77
  50.2 29.1 %collective-permute-start.3 = (bf16[688,512]{1,0:T(8,128)(2,1)S(1)}, bf16[688,512]{1,0:T(8,128)(2,1)}, u32[]{:S(2)}, u32[]{:S(2)}) collective-permute-start(bf16[688,512]{1,0:T(8,128)(2,1)S(1)} %get-tuple-element.62), channel_id=1, source_target_pairs={{0,8},{8,16},{16,24},{24,0},{1,9},{9,17},{17,25},{25,1},{2,10},{10... | collective-permute-start | bytes 2113544 | tf_op jit(solution)/shard_map/ppermute | solution.py:77
  79.2 45.1 %collective-permute-done.1 = bf16[688,512]{1,0:T(8,128)(2,1)} collective-permute-done((bf16[688,512]{1,0:T(8,128)(2,1)}, bf16[688,512]{1,0:T(8,128)(2,1)}, u32[]{:S(2)}, u32[]{:S(2)}) %collective-permute-start.1) | collective-permute-done | bytes 704544 | tf_op jit(solution)/shard_map/ppermute | solution.py:77
  139.7 10.8 %collective-permute-done.4 = bf16[688,512]{1,0:T(8,128)(2,1)} collective-permute-done((bf16[688,512]{1,0:T(8,128)(2,1)}, bf16[688,512]{1,0:T(8,128)(2,1)}, u32[]{:S(2)}, u32[]{:S(2)}) %collective-permute-start.4) | collective-permute-done | bytes 704544 | tf_op jit(solution)/shard_map/ppermute | solution.py:77
  164.1 44.2 %all-gather.9.cloned.1.call-done = bf16[1024,1024]{1,0:T(8,128)(2,1)} async-done(((bf16[256,1024]{1,0:T(8,128)(2,1)}), bf16[1024,1024]{1,0:T(8,128)(2,1)}) %all-gather.9.cloned.1.call-update) | async-done | bytes 2097168 | tf_op jit(solution)/shard_map/all_gather | solution.py:115
  214.8 5.2 %all-to-all-start = ((bf16[4,576,1024]{2,1,0:T(8,128)(2,1)}), bf16[4,576,1024]{2,1,0:T(8,128)(2,1)}, u32[]{:S(2)}, u32[]{:S(2)}) async-start(bf16[4,576,1024]{2,1,0:T(8,128)(2,1)} %pad_maximum_fusion.3), calls=%async_computation | async-start | bytes 9437184 | tf_op jit(solution)/shard_map/all_to_all | solution.py:133
  223.5 15.5 %collective-permute-done.8 = bf16[688,512]{1,0:T(8,128)(2,1)S(1)} collective-permute-done((bf16[688,512]{1,0:T(8,128)(2,1)S(1)}, bf16[688,512]{1,0:T(8,128)(2,1)S(1)}, u32[]{:S(2)}, u32[]{:S(2)}) %collective-permute-start.8) | collective-permute-done | bytes 704544 | tf_op jit(solution)/shard_map/ppermute | solution.py:77
  238.9 43.6 %collective-permute-done.7 = bf16[688,512]{1,0:T(8,128)(2,1)S(1)} collective-permute-done((bf16[688,512]{1,0:T(8,128)(2,1)S(1)}, bf16[688,512]{1,0:T(8,128)(2,1)S(1)}, u32[]{:S(2)}, u32[]{:S(2)}) %collective-permute-start.7) | collective-permute-done | bytes 704544 | tf_op jit(solution)/shard_map/ppermute | solution.py:77
  285.2 6.5 %reshape.189 = bf16[2,2,512,688]{2,1,0,3:T(2,128)(2,1)S(1)} reshape(bf16[2048,688]{0,1:T(8,128)(2,1)} %maximum_bitcast_fusion.2) | data formatting | bytes 5636096 | tf_op jit(solution)/shard_map/reshape | solution.py:146
  291.7 19.3 %slice_reduce_fusion.1 = (bf16[2,512,688]{1,0,2:T(2,128)(2,1)S(1)}, bf16[2,512,688]{1,0,2:T(2,128)(2,1)}) fusion(bf16[2,2,512,688]{2,1,0,3:T(2,128)(2,1)S(1)} %reshape.189), kind=kLoop, calls=%fused_computation.18 | loop fusion | bytes 5636096 | tf_op jit(solution)/shard_map/slice | solution.py:152
  312.5 7.3 %fusion.99 = (bf16[2304,1024]{1,0:T(8,128)(2,1)S(1)}, bf16[2304,1024]{1,0:T(8,128)(2,1)}) fusion(bf16[4608,1024]{1,0:T(8,128)(2,1)} %all-gather.11.cloned.1.call-done), kind=kLoop, calls=%fused_computation.212 | loop fusion | bytes 18874368 | tf_op jit(solution)/shard_map/slice | solution.py:139
  319.8 11.6 %fusion.1 = f32[2304,688]{0,1:T(8,128)} fusion(bf16[2048,688]{0,1:T(8,128)(2,1)S(1)} %copy-done.12, bf16[2304,1024]{1,0:T(8,128)(2,1)} %get-tuple-element.44, bf16[2304,1024]{1,0:T(8,128)(2,1)S(1)} %get-tuple-element.43), kind=kOutput, calls=%fused_computation.5 | convolution fusion | flops 6511656960 | bytes 18595840 | tf_op jit(solution)/shard_map/dot_general | solution.py:141
  331.4 9.6 %multiply_convert_fusion = bf16[2304,688]{0,1:T(8,128)(2,1)S(1)} fusion(f32[2304,688]{0,1:T(8,128)} %fusion.1, bf16[2048,688]{0,1:T(8,128)(2,1)S(1)} %copy-done.11, bf16[2304,1024]{1,0:T(8,128)(2,1)S(1)} %copy-done.8, bf16[2304,1024]{1,0:T(8,128)(2,1)S(1)} %get-tuple-element.43), kind=kOutput, calls=%fused_computation.4 | convolution fusion | flops 6521167872 | bytes 21766144 | tf_op jit(solution)/shard_map/dot_general | solution.py:140
  342.7 5.5 %convolution_convert_fusion.1 = bf16[2304,1024]{1,0:T(8,128)(2,1)} fusion(bf16[2304,688]{0,1:T(8,128)(2,1)S(1)} %multiply_convert_fusion, bf16[1024,688]{0,1:T(8,128)(2,1)S(1)} %bitcast.174), kind=kOutput, calls=%fused_computation.10 | convolution fusion | flops 3248750592 | bytes 9297920 | tf_op jit(solution)/shard_map/dot_general | solution.py:150
  349.9 7.6 %convolution_convert_fusion = bf16[2304,1024]{1,0:T(8,128)(2,1)} fusion(bf16[2304,688]{0,1:T(8,128)(2,1)} %copy-done.20, bf16[1024,688]{0,1:T(8,128)(2,1)S(1)} %bitcast.175), kind=kOutput, calls=%fused_computation.9 | convolution fusion | flops 3248750592 | bytes 9297920 | tf_op jit(solution)/shard_map/dot_general | solution.py:150
  357.5 4.2 reduce-scatter.5.cloned.1.call-done
  361.7 3.9 all-to-all-start.1
  366.2 11.4 %reduce-scatter.9.cloned.1.call-done = bf16[2304,512]{1,0:T(8,128)(2,1)} async-done(((bf16[2304,1024]{1,0:T(8,128)(2,1)}), bf16[2304,512]{1,0:T(8,128)(2,1)}) %reduce-scatter.9.cloned.1.call-update) | async-done | bytes 2359312 | tf_op jit(solution)/shard_map/reduce_scatter | solution.py:156
  377.7 16.1 %all-to-all-done.1 = bf16[4,576,512]{2,1,0:T(8,128)(2,1)S(1)} async-done(((bf16[4,576,512]{2,1,0:T(8,128)(2,1)}), bf16[4,576,512]{2,1,0:T(8,128)(2,1)S(1)}, u32[]{:S(2)}, u32[]{:S(2)}) %all-to-all-start.1) | async-done | bytes 2359328 | tf_op jit(solution)/shard_map/all_to_all | solution.py:157
  395.2 3.6 all-to-all-start.2
  405.4 20.7 %all-to-all-done.2 = bf16[4,576,512]{2,1,0:T(8,128)(2,1)S(1)} async-done(((bf16[4,576,512]{2,1,0:T(8,128)(2,1)}), bf16[4,576,512]{2,1,0:T(8,128)(2,1)S(1)}, u32[]{:S(2)}, u32[]{:S(2)}) %all-to-all-start.2) | async-done | bytes 2359328 | tf_op jit(solution)/shard_map/all_to_all | solution.py:157
  430.8 3.5 reduce-scatter.7.cloned.1.call-done
  434.3 28.1 %reduce-scatter.11.cloned.1.call-done = bf16[256,512]{1,0:T(8,128)(2,1)} async-done(((bf16[1024,512]{1,0:T(8,128)(2,1)}), bf16[256,512]{1,0:T(8,128)(2,1)}) %reduce-scatter.11.cloned.1.call-update) | async-done | bytes 262160 | tf_op jit(solution)/shard_map/reduce_scatter | solution.py:179
  (152 shorter events, 78.3 us)
Async XLA Ops:
  6.5 124.2 %copy-start = (bf16[256,1024]{1,0:T(8,128)(2,1)S(1)}, bf16[256,1024]{1,0:T(8,128)(2,1)}, u32[]{:S(2)}) copy-start(bf16[256,1024]{1,0:T(8,128)(2,1)} %param.12) | copy-start | bytes 1572868
  6.5 121.5 %all-gather.7.cloned.1.call-start = ((), (), s32[]{:S(2)}) async-start(), calls=%async_computation.7 | async-start | bytes 5242880 | tf_op jit(solution)/shard_map/all_gather | solution.py:89
  10.2 146.9 %all-reduce.2.cloned.1.call-start = ((), (), s32[]{:S(2)}) async-start(), calls=%async_computation.8 | async-start | bytes 2097152 | tf_op jit(solution)/shard_map/psum | solution.py:101
  25.4 138.0 %copy-start.2 = (f32[1024,4]{1,0:T(8,128)}, f32[1024,4]{1,0:T(8,128)S(1)}, u32[]{:S(2)}) copy-start(f32[1024,4]{1,0:T(8,128)S(1)} %copy.23) | copy-start | bytes 49156
  28.8 21.4 %collective-permute-start.2 = (bf16[688,512]{1,0:T(8,128)(2,1)}, bf16[688,512]{1,0:T(8,128)(2,1)}, u32[]{:S(2)}, u32[]{:S(2)}) collective-permute-start(bf16[688,512]{1,0:T(8,128)(2,1)} %get-tuple-element.68), channel_id=1, source_target_pairs={{0,24},{8,0},{16,8},{24,16},{1,25},{9,1},{17,9},{25,17},{2,26},{10... | collective-permute-start | bytes 2113544 | tf_op jit(solution)/shard_map/ppermute | solution.py:77
  32.2 92.2 %collective-permute-start.1 = (bf16[688,512]{1,0:T(8,128)(2,1)}, bf16[688,512]{1,0:T(8,128)(2,1)}, u32[]{:S(2)}, u32[]{:S(2)}) collective-permute-start(bf16[688,512]{1,0:T(8,128)(2,1)} %get-tuple-element.69), channel_id=1, source_target_pairs={{0,16},{8,24},{16,0},{24,8},{1,17},{9,25},{17,1},{25,9},{2,18},{10... | collective-permute-start | bytes 2113544 | tf_op jit(solution)/shard_map/ppermute | solution.py:77
  32.2 92.2 %collective-permute-start = (bf16[688,512]{1,0:T(8,128)(2,1)}, bf16[688,512]{1,0:T(8,128)(2,1)}, u32[]{:S(2)}, u32[]{:S(2)}) collective-permute-start(bf16[688,512]{1,0:T(8,128)(2,1)} %get-tuple-element.70), channel_id=1, source_target_pairs={{0,8},{8,16},{16,24},{24,0},{1,9},{9,17},{17,25},{25,1},{2,10},{10... | collective-permute-start | bytes 2113544 | tf_op jit(solution)/shard_map/ppermute | solution.py:77
  34.1 105.6 %collective-permute-start.5 = (bf16[688,512]{1,0:T(8,128)(2,1)}, bf16[688,512]{1,0:T(8,128)(2,1)}, u32[]{:S(2)}, u32[]{:S(2)}) collective-permute-start(bf16[688,512]{1,0:T(8,128)(2,1)} %get-tuple-element.60), channel_id=1, source_target_pairs={{0,24},{8,0},{16,8},{24,16},{1,25},{9,1},{17,9},{25,17},{2,26},{10... | collective-permute-start | bytes 2113544 | tf_op jit(solution)/shard_map/ppermute | solution.py:77
  37.4 113.2 %collective-permute-start.4 = (bf16[688,512]{1,0:T(8,128)(2,1)}, bf16[688,512]{1,0:T(8,128)(2,1)}, u32[]{:S(2)}, u32[]{:S(2)}) collective-permute-start(bf16[688,512]{1,0:T(8,128)(2,1)} %get-tuple-element.61), channel_id=1, source_target_pairs={{0,16},{8,24},{16,0},{24,8},{1,17},{9,25},{17,1},{25,9},{2,18},{10... | collective-permute-start | bytes 2113544 | tf_op jit(solution)/shard_map/ppermute | solution.py:77
  50.2 100.4 %collective-permute-start.3 = (bf16[688,512]{1,0:T(8,128)(2,1)S(1)}, bf16[688,512]{1,0:T(8,128)(2,1)}, u32[]{:S(2)}, u32[]{:S(2)}) collective-permute-start(bf16[688,512]{1,0:T(8,128)(2,1)S(1)} %get-tuple-element.62), channel_id=1, source_target_pairs={{0,8},{8,16},{16,24},{24,0},{1,9},{9,17},{17,25},{25,1},{2,10},{10... | collective-permute-start | bytes 2113544 | tf_op jit(solution)/shard_map/ppermute | solution.py:77
  139.1 69.2 %all-gather.9.cloned.1.call-start = ((), (), s32[]{:S(2)}) async-start(), calls=%async_computation.13 | async-start | bytes 2621440 | tf_op jit(solution)/shard_map/all_gather | solution.py:115
  214.8 70.1 %all-to-all-start = ((bf16[4,576,1024]{2,1,0:T(8,128)(2,1)}), bf16[4,576,1024]{2,1,0:T(8,128)(2,1)}, u32[]{:S(2)}, u32[]{:S(2)}) async-start(bf16[4,576,1024]{2,1,0:T(8,128)(2,1)} %pad_maximum_fusion.3), calls=%async_computation | async-start | bytes 9437184 | tf_op jit(solution)/shard_map/all_to_all | solution.py:133
  220.0 92.5 %all-gather.11.cloned.1.call-start = ((), (), s32[]{:S(2)}) async-start(), calls=%async_computation.14 | async-start | bytes 14155776 | tf_op jit(solution)/shard_map/all_gather | solution.py:138
  220.3 18.6 %collective-permute-start.8 = (bf16[688,512]{1,0:T(8,128)(2,1)S(1)}, bf16[688,512]{1,0:T(8,128)(2,1)S(1)}, u32[]{:S(2)}, u32[]{:S(2)}) collective-permute-start(bf16[688,512]{1,0:T(8,128)(2,1)S(1)} %get-tuple-element.52), channel_id=1, source_target_pairs={{0,24},{8,0},{16,8},{24,16},{1,25},{9,1},{17,9},{25,17},{2,26},{10... | collective-permute-start | bytes 2113544 | tf_op jit(solution)/shard_map/ppermute | solution.py:77
  221.5 61.0 %collective-permute-start.7 = (bf16[688,512]{1,0:T(8,128)(2,1)S(1)}, bf16[688,512]{1,0:T(8,128)(2,1)S(1)}, u32[]{:S(2)}, u32[]{:S(2)}) collective-permute-start(bf16[688,512]{1,0:T(8,128)(2,1)S(1)} %get-tuple-element.53), channel_id=1, source_target_pairs={{0,16},{8,24},{16,0},{24,8},{1,17},{9,25},{17,1},{25,9},{2,18},{10... | collective-permute-start | bytes 2113544 | tf_op jit(solution)/shard_map/ppermute | solution.py:77
  221.7 60.8 %collective-permute-start.6 = (bf16[688,512]{1,0:T(8,128)(2,1)S(1)}, bf16[688,512]{1,0:T(8,128)(2,1)S(1)}, u32[]{:S(2)}, u32[]{:S(2)}) collective-permute-start(bf16[688,512]{1,0:T(8,128)(2,1)S(1)} %get-tuple-element.54), channel_id=1, source_target_pairs={{0,8},{8,16},{16,24},{24,0},{1,9},{9,17},{17,25},{25,1},{2,10},{10... | collective-permute-start | bytes 2113544 | tf_op jit(solution)/shard_map/ppermute | solution.py:77
  285.0 76.7 %reduce-scatter.5.cloned.1.call-start = ((), (), s32[]{:S(2)}) async-start(), calls=%async_computation.9 | async-start | bytes 7077888 | tf_op jit(solution)/shard_map/reduce_scatter | solution.py:156
  348.2 29.4 %reduce-scatter.9.cloned.1.call-start = ((), (), s32[]{:S(2)}) async-start(), calls=%async_computation.11 | async-start | bytes 7077888 | tf_op jit(solution)/shard_map/reduce_scatter | solution.py:156
  361.7 32.0 %all-to-all-start.1 = ((bf16[4,576,512]{2,1,0:T(8,128)(2,1)}), bf16[4,576,512]{2,1,0:T(8,128)(2,1)S(1)}, u32[]{:S(2)}, u32[]{:S(2)}) async-start(bf16[4,576,512]{2,1,0:T(8,128)(2,1)} %bitcast.172), calls=%async_computation.2 | async-start | bytes 4718592 | tf_op jit(solution)/shard_map/all_to_all | solution.py:157
  395.2 30.9 %all-to-all-start.2 = ((bf16[4,576,512]{2,1,0:T(8,128)(2,1)}), bf16[4,576,512]{2,1,0:T(8,128)(2,1)S(1)}, u32[]{:S(2)}, u32[]{:S(2)}) async-start(bf16[4,576,512]{2,1,0:T(8,128)(2,1)} %bitcast.171), calls=%async_computation.5 | async-start | bytes 4718592 | tf_op jit(solution)/shard_map/all_to_all | solution.py:157
  398.8 35.5 %reduce-scatter.7.cloned.1.call-start = ((), (), s32[]{:S(2)}) async-start(), calls=%async_computation.10 | async-start | bytes 1310720 | tf_op jit(solution)/shard_map/reduce_scatter | solution.py:179
  405.4 57.0 %reduce-scatter.11.cloned.1.call-start = ((), (), s32[]{:S(2)}) async-start(), calls=%async_computation.12 | async-start | bytes 1310720 | tf_op jit(solution)/shard_map/reduce_scatter | solution.py:179
  429.2 33.2 %copy-start.6 = (f32[256,2048]{1,0:T(8,128)S(1)}, f32[256,2048]{1,0:T(8,128)}, u32[]{:S(2)}) copy-start(f32[256,2048]{1,0:T(8,128)} %copy-done.5) | copy-start | bytes 6291460
  429.2 35.2 %copy-start.1 = (bf16[256,1024]{1,0:T(8,128)(2,1)S(1)}, bf16[256,1024]{1,0:T(8,128)(2,1)}, u32[]{:S(2)}) copy-start(bf16[256,1024]{1,0:T(8,128)(2,1)} %param.12) | copy-start | bytes 1572868
  (17 other events, 88.7 us)
Sparse Core Ops, SparseCore 0:
  10.3 55.2 all-gather.6
  139.2 17.7 all-reduce.1
  161.1 47.1 all-gather.8
  285.1 22.5 all-gather.10
  348.3 13.3 reduce-scatter.4
  363.9 13.7 reduce-scatter.8
  405.5 28.7 reduce-scatter.6
  436.6 25.7 reduce-scatter.10
